TPU v7x, 768 devices: a whole 4x8x12 slice. The times are simulated.
768 devices in a mesh: outer: 16 (over x_hi, y), inner: 48 (over z, x_lo, core).
Axes of the slice: x: 4 (x_hi: 2, x_lo: 2; x = x_hi * 2 + x_lo), y: 8, z: 12, core: 2. Of those that a mesh axis runs over, the one named last changes fastest.
Arguments:
- layer_input: bfloat16 [147456, 8192], P(('outer', 'inner')), may hold values from -6 to 6
- query: bfloat16 [147456, 1024], P(('outer', 'inner')), may hold values from -5 to 5
- keys_values: bfloat16 [147456, 256], P(('outer', 'inner')), may hold values from -5 to 5
- grad_output: bfloat16 [147456, 1024], P(('outer', 'inner')), may hold values from -48 to 48
- logsumexp: float32 [147456, 8], P(('outer', 'inner')), as said below
- delta: float32 [147456, 8], P(('outer', 'inner')), may hold values from -192 to 192
Outputs:
- grad_query: bfloat16 [147456, 1024], P(('outer', 'inner'))
- grad_keys_values: bfloat16 [147456, 256], P(('outer', 'inner'))
- grad_weight: float32 [8192, 256], P('outer')
Inputs may be any that keep to these rules, and one draw needn't show every extreme that they name: logsumexp[i, h] exceeds the log-sum-exp of row i's scores over its allowed keys, so that every probs entry is below 1.
All inputs are finite; a program needn't handle non-finite values.
Results may differ from a plain program's by a relative error of at most 0.018.
Values may be sent and summed in bfloat16 or wider, within the bound.
A program may use at most 64 MiB of HBM per device.

v0:
```python
import jax
import jax.numpy as jnp
from jax import lax
from jax.sharding import Mesh
from jax.sharding import PartitionSpec as P

HD = 128
HQ = 8
WIN = 3
OUTER = ("outer_0", "outer_1")
OUTER_INNER = ("outer_0", "outer_1", "inner")


def shifted(value, axis, steps):
    count = lax.axis_size(axis)
    first, last = (max(0, -steps), min(count, count - steps))
    return lax.ppermute(value, axis, [(source, source + steps) for source in range(first, last)])


def sum_in_order(parts, axes, order):
    dims = [lax.axis_size(a) for a in axes]
    parts = parts.reshape(*dims, *parts.shape[1:])
    parts = parts.transpose(*order, *range(len(axes), parts.ndim))
    parts = parts.reshape(-1, *parts.shape[len(axes) :])
    for k in order:
        parts = lax.psum_scatter(parts, axes[k], scatter_dimension=0, tiled=True)
    return parts[0]


def cut_along(value, dim, size):
    dims = value.shape
    parts = value.reshape(*dims[:dim], size, dims[dim] // size, *dims[dim + 1 :])
    return jnp.moveaxis(parts, dim, 0)


def summed_rows_2(value, axes, order, dim):
    size = lax.axis_size(axes)
    return sum_in_order(cut_along(value, dim, size), axes, order)


def filled_up(lines, size):
    spare = -len(lines) % size
    return jnp.pad(lines, [(0, spare)] + [(0, 0)] * (lines.ndim - 1))


def total_of(value, axis):
    lines = value.reshape(-1, *value.shape[1:][-1:])
    own = lax.psum_scatter(
        filled_up(lines, lax.axis_size(axis)), axis, scatter_dimension=0, tiled=True
    )
    whole = lax.all_gather(own, axis).reshape(-1, *lines.shape[1:])
    return lax.slice_in_dim(whole, 0, len(lines)).reshape(value.shape)


def make_allowed(tok_rows, inner_pos, outer_pos):
    query_pos = lax.broadcasted_iota(jnp.int32, (tok_rows, (WIN + 2) * tok_rows), 0)
    column = lax.broadcasted_iota(jnp.int32, (tok_rows, (WIN + 2) * tok_rows), 1)
    key_slot = column // tok_rows
    key_pos = column % tok_rows
    own_block = (key_slot == 0) & (key_pos <= query_pos)
    near_block = (key_slot >= 1) & (key_slot <= WIN) & (inner_pos >= key_slot)
    memory_block = (key_slot == WIN + 1) & (outer_pos >= 1)
    return own_block | near_block | memory_block


def local_grads(query, key_rows_all, grad_output, logsumexp, delta, inner_pos, outer_pos):
    tok_rows = query.shape[0]
    scaling = HD ** (-0.5)
    query_heads = query.reshape(tok_rows, HQ, HD)
    grad_heads = grad_output.reshape(tok_rows, HQ, HD)
    key_rows = key_rows_all[:, :HD]
    value_rows = key_rows_all[:, HD:]
    scores = (
        jnp.einsum("thd,kd->htk", query_heads, key_rows, preferred_element_type=jnp.float32)
        * scaling
    )
    allowed = make_allowed(tok_rows, inner_pos, outer_pos)
    scores = jnp.where(allowed[None], scores, -jnp.inf)
    probs = jnp.exp(scores - jnp.transpose(logsumexp)[:, :, None])
    probs_half = probs.astype(jnp.bfloat16)
    grad_probs = jnp.einsum(
        "thd,kd->htk", grad_heads, value_rows, preferred_element_type=jnp.float32
    )
    grad_scores = (probs * (grad_probs - jnp.transpose(delta)[:, :, None]) * scaling).astype(
        jnp.bfloat16
    )
    grad_query = jnp.einsum(
        "htk,kd->thd", grad_scores, key_rows, preferred_element_type=jnp.float32
    )
    grad_query = grad_query.reshape(tok_rows, HQ * HD).astype(jnp.bfloat16)
    grad_keys = jnp.einsum(
        "htk,thd->kd", grad_scores, query_heads, preferred_element_type=jnp.float32
    )
    grad_values = jnp.einsum(
        "htk,thd->kd", probs_half, grad_heads, preferred_element_type=jnp.float32
    )
    return (grad_query, jnp.concatenate([grad_keys, grad_values], axis=-1))


def local(layer_input, query, keys_values, grad_output, logsumexp, delta):
    tok_rows = query.shape[0]
    inner_pos = lax.axis_index("inner")
    outer_pos = lax.axis_index(OUTER)
    blocks = [keys_values]
    moving = keys_values
    for offset in range(WIN):
        moving = shifted(moving, "inner", 1)
        blocks.append(moving)
    memory = shifted(keys_values, OUTER, 1)
    key_rows_all = jnp.concatenate(blocks + [memory], axis=0)
    grad_query, grad_terms = local_grads(
        query, key_rows_all, grad_output, logsumexp, delta, inner_pos, outer_pos
    )
    pieces = grad_terms.reshape(WIN + 2, tok_rows, 2 * HD)
    relayed = pieces[WIN]
    for offset in range(WIN - 1, -1, -1):
        relayed = shifted(relayed.astype(jnp.bfloat16), "inner", -1).astype(relayed.dtype)
        if offset > 0:
            relayed = relayed + pieces[offset]
    summed = pieces[0] + relayed
    summed = summed + shifted(pieces[WIN + 1].astype(jnp.bfloat16), OUTER, -1).astype(jnp.float32)
    grad_kv = summed.astype(jnp.bfloat16)
    shared_rows = summed_rows_2(
        lax.dot_general(
            layer_input, grad_kv, (((0,), (0,)), ((), ())), preferred_element_type=jnp.float32
        ).astype(jnp.bfloat16),
        OUTER,
        (1, 0),
        0,
    ).astype(jnp.float32)
    grad_weight = total_of(shared_rows, "inner")
    return (grad_query, grad_kv, grad_weight)


def solution(mesh):
    finer = Mesh(mesh.devices.reshape(2, 8, mesh.shape["inner"]), ("outer_0", "outer_1", "inner"))
    return jax.shard_map(
        local,
        mesh=finer,
        in_specs=(
            P(OUTER_INNER, None),
            P(OUTER_INNER, None),
            P(OUTER_INNER, None),
            P(OUTER_INNER, None),
            P(OUTER_INNER, None),
            P(OUTER_INNER, None),
        ),
        out_specs=(P(OUTER_INNER, None), P(OUTER_INNER, None), P(OUTER, None)),
        check_vma=False,
    )
```

profile of v0, /device:TPU:1, one launch (start us, length us, event | category | flops | bytes accessed | tf_op | source)
XLA Modules:
  0.0 386.0 jit_solution(10258825082027867418)
XLA Ops:
  7.2 4.8 %collective-permute-start = (bf16[192,256]{1,0:T(8,128)(2,1)}, bf16[192,256]{1,0:T(8,128)(2,1)S(1)}, u32[]{:S(2)}, u32[]{:S(2)}) collective-permute-start(bf16[192,256]{1,0:T(8,128)(2,1)} %param.8), channel_id=1, source_target_pairs={{0,1},{1,2},{2,3},{3,4},{4,5},{5,6},{6,7},{7,8},{8,9},{9,10},{10,1... | collective-permute-start | bytes 294920 | tf_op jit(solution)/shard_map/ppermute | solution.py:17
  12.0 3.2 collective-permute-start.3
  16.4 3.9 collective-permute-done
  23.9 4.2 %collective-permute-start.2 = (bf16[192,256]{1,0:T(8,128)(2,1)S(1)}, bf16[192,256]{1,0:T(8,128)(2,1)S(1)}, u32[]{:S(2)}, u32[]{:S(2)}) collective-permute-start(bf16[192,256]{1,0:T(8,128)(2,1)S(1)} %collective-permute-done.1), channel_id=1, source_target_pairs={{0,1},{1,2},{2,3},{3,4},{4,5},{5,6},{6,7},{7,8},{8,9},{9,10},{10,1... | collective-permute-start | bytes 294920 | tf_op jit(solution)/shard_map/ppermute | solution.py:17
  39.3 4.7 %collective-permute-done.4 = bf16[192,256]{1,0:T(8,128)(2,1)S(1)} collective-permute-done((bf16[192,256]{1,0:T(8,128)(2,1)S(1)}, bf16[192,256]{1,0:T(8,128)(2,1)S(1)}, u32[]{:S(2)}, u32[]{:S(2)}) %collective-permute-start.4) | collective-permute-done | bytes 98336 | tf_op jit(solution)/shard_map/ppermute | solution.py:17
  47.3 2.7 collective-permute-done.5
  51.9 4.0 %collective-permute-done.6 = bf16[192,256]{1,0:T(8,128)(2,1)S(1)} collective-permute-done((bf16[192,256]{1,0:T(8,128)(2,1)S(1)}, bf16[192,256]{1,0:T(8,128)(2,1)S(1)}, u32[]{:S(2)}, u32[]{:S(2)}) %collective-permute-start.6) | collective-permute-done | bytes 98336 | tf_op jit(solution)/shard_map/ppermute | solution.py:17
  57.3 3.9 %copy.28 = bf16[32,8,16,512]{3,2,1,0:T(8,128)(2,1)} copy(bf16[32,8,16,512]{3,1,2,0:T(8,128)(2,1)S(1)} %bitcast.83) | data formatting | bytes 8388608
  61.1 7.5 %copy.24 = bf16[2,8,512,256]{3,2,0,1:T(8,128)(2,1)} copy(bf16[2,8,512,256]{2,1,0,3:T(8,128)(2,1)} %bitcast.85) | data formatting | bytes 8388608 | tf_op jit(solution)/shard_map/reshape;reshape | solution.py:22
  68.8 73.2 %reduce-scatter.5.cloned.1.call-done = bf16[2,512,256]{2,1,0:T(8,128)(2,1)} async-done(((bf16[16,512,256]{2,1,0:T(8,128)(2,1)}), bf16[2,512,256]{2,1,0:T(8,128)(2,1)}) %reduce-scatter.5.cloned.1.call-update) | async-done | bytes 524304 | tf_op jit(solution)/shard_map/reduce_scatter | solution.py:26
  142.0 28.8 %reduce-scatter.7.cloned.1.call-done = bf16[1,512,256]{2,1,0:T(8,128)(2,1)} async-done(((bf16[2,512,256]{2,1,0:T(8,128)(2,1)}), bf16[1,512,256]{2,1,0:T(8,128)(2,1)}) %reduce-scatter.7.cloned.1.call-update) | async-done | bytes 262160 | tf_op jit(solution)/shard_map/reduce_scatter | solution.py:26
  172.6 83.7 %fusion = f32[16,256]{1,0:T(8,128)S(1)} fusion(f32[528,256]{1,0:T(8,128)} %pad_convert_fusion), kind=kCustom, calls=%all-reduce-scatter | all-reduce-scatter fusion | flops 196609 | bytes 561152
  256.3 4.6 %collective-permute-start.21 = (f32[16,256]{1,0:T(8,128)S(1)}, f32[16,256]{1,0:T(8,128)S(1)}, u32[]{:S(2)}, u32[]{:S(2)}) collective-permute-start(f32[16,256]{1,0:T(8,128)S(1)} %fusion), channel_id=1, source_target_pairs={{0,14},{1,15},{2,16},{3,17},{4,18},{5,19},{6,20},{7,21},{8,22},{9,... | collective-permute-start | bytes 49160
  260.9 4.3 %collective-permute-start.20 = (f32[16,256]{1,0:T(8,128)S(1)}, f32[16,256]{1,0:T(8,128)S(1)}, u32[]{:S(2)}, u32[]{:S(2)}) collective-permute-start(f32[16,256]{1,0:T(8,128)S(1)} %fusion), channel_id=1, source_target_pairs={{0,13},{1,14},{2,15},{3,16},{4,17},{5,18},{6,19},{7,20},{8,21},{9,... | collective-permute-start | bytes 49160
  267.9 5.3 %collective-permute-start.22 = (f32[11,256]{1,0:T(8,128)S(1)}, f32[11,256]{1,0:T(8,128)S(1)}, u32[]{:S(2)}, u32[]{:S(2)}) collective-permute-start(f32[11,256]{1,0:T(8,128)S(1)} %slice.51), channel_id=1, source_target_pairs={{0,15},{1,16},{2,17},{3,18},{4,19},{5,20},{6,21},{7,22},{8,23},{9,... | collective-permute-start | bytes 33800
  274.1 3.0 collective-permute-start.17
  277.1 13.6 %collective-permute-start.16 = (f32[16,256]{1,0:T(8,128)S(1)}, f32[16,256]{1,0:T(8,128)S(1)}, u32[]{:S(2)}, u32[]{:S(2)}) collective-permute-start(f32[16,256]{1,0:T(8,128)S(1)} %fusion), channel_id=1, source_target_pairs={{0,9},{1,10},{2,11},{3,12},{4,13},{5,14},{6,15},{7,16},{8,17},{9,1... | collective-permute-start | bytes 49160
  294.0 3.5 collective-permute-start.13
  301.8 2.8 collective-permute-start.11
  306.0 3.1 collective-permute-start.9
  309.1 3.4 collective-permute-start.8
  312.5 3.0 fusion.13
  317.6 6.4 %concatenate.8 = f32[251,256]{1,0:T(8,128)S(1)} concatenate(f32[11,256]{1,0:T(8,128)S(1)} %collective-permute-done.22, f32[16,256]{1,0:T(8,128)S(1)} %collective-permute-done.21, f32[16,256]{1,0:T(8,128)S(1)} %collective-permute-done.20, f32[16,256]{1,0:T(8,128)S(1)} %collective-permute-done.19, f32[16,256]{1,0:T(8,128)S(1)} %collective-permute-done.18, ...), dimensions={0} | concatenate | bytes 514048
  324.1 51.2 %all-gather.1 = f32[48,11,256]{2,1,0:T(8,128)} all-gather(f32[1,11,256]{2,1,0:T(8,128)S(1)} %dynamic-slice_bitcast_fusion), channel_id=2, replica_groups=mesh['outer_0'=2,'outer_1'=8,'inner'=48] {'inner'}, dimensions={0}, use_global_device_ids=true | all-gather | bytes 551936 | tf_op jit(solution)/shard_map/all_gather | solution.py:51
  (88 shorter events, 41.9 us)
Async XLA Ops:
  7.2 134.8 %reduce-scatter.5.cloned.1.call-start = ((), (), s32[]{:S(2)}) async-start(), calls=%async_computation.2 | async-start | bytes 4718592 | tf_op jit(solution)/shard_map/reduce_scatter | solution.py:26
  7.2 13.1 %collective-permute-start = (bf16[192,256]{1,0:T(8,128)(2,1)}, bf16[192,256]{1,0:T(8,128)(2,1)S(1)}, u32[]{:S(2)}, u32[]{:S(2)}) collective-permute-start(bf16[192,256]{1,0:T(8,128)(2,1)} %param.8), channel_id=1, source_target_pairs={{0,1},{1,2},{2,3},{3,4},{4,5},{5,6},{6,7},{7,8},{8,9},{9,10},{10,1... | collective-permute-start | bytes 294920 | tf_op jit(solution)/shard_map/ppermute | solution.py:17
  12.0 17.8 %collective-permute-start.3 = (bf16[192,256]{1,0:T(8,128)(2,1)}, bf16[192,256]{1,0:T(8,128)(2,1)S(1)}, u32[]{:S(2)}, u32[]{:S(2)}) collective-permute-start(bf16[192,256]{1,0:T(8,128)(2,1)} %param.8), channel_id=1, source_target_pairs={{0,48},{48,96},{96,144},{144,192},{192,240},{240,288},{288,336},{3... | collective-permute-start | bytes 294920 | tf_op jit(solution)/shard_map/ppermute | solution.py:17
  23.9 5.8 %collective-permute-start.2 = (bf16[192,256]{1,0:T(8,128)(2,1)S(1)}, bf16[192,256]{1,0:T(8,128)(2,1)S(1)}, u32[]{:S(2)}, u32[]{:S(2)}) collective-permute-start(bf16[192,256]{1,0:T(8,128)(2,1)S(1)} %collective-permute-done.1), channel_id=1, source_target_pairs={{0,1},{1,2},{2,3},{3,4},{4,5},{5,6},{6,7},{7,8},{8,9},{9,10},{10,1... | collective-permute-start | bytes 294920 | tf_op jit(solution)/shard_map/ppermute | solution.py:17
  37.4 6.6 %collective-permute-start.4 = (bf16[192,256]{1,0:T(8,128)(2,1)S(1)}, bf16[192,256]{1,0:T(8,128)(2,1)S(1)}, u32[]{:S(2)}, u32[]{:S(2)}) collective-permute-start(bf16[192,256]{1,0:T(8,128)(2,1)S(1)} %get-tuple-element.3), channel_id=1, source_target_pairs={{1,0},{2,1},{3,2},{4,3},{5,4},{6,5},{7,6},{8,7},{9,8},{10,9},{11,1... | collective-permute-start | bytes 294920 | tf_op jit(solution)/shard_map/ppermute | solution.py:17
  44.0 5.9 %collective-permute-start.5 = (bf16[192,256]{1,0:T(8,128)(2,1)S(1)}, bf16[192,256]{1,0:T(8,128)(2,1)S(1)}, u32[]{:S(2)}, u32[]{:S(2)}) collective-permute-start(bf16[192,256]{1,0:T(8,128)(2,1)S(1)} %fusion.36), channel_id=1, source_target_pairs={{1,0},{2,1},{3,2},{4,3},{5,4},{6,5},{7,6},{8,7},{9,8},{10,9},{11,1... | collective-permute-start | bytes 294920 | tf_op jit(solution)/shard_map/ppermute | solution.py:17
  46.0 6.0 %collective-permute-start.7 = (bf16[192,256]{1,0:T(8,128)(2,1)S(1)}, bf16[192,256]{1,0:T(8,128)(2,1)S(1)}, u32[]{:S(2)}, u32[]{:S(2)}) collective-permute-start(bf16[192,256]{1,0:T(8,128)(2,1)S(1)} %get-tuple-element.4), channel_id=1, source_target_pairs={{48,0},{96,48},{144,96},{192,144},{240,192},{288,240},{336,288},{3... | collective-permute-start | bytes 294920 | tf_op jit(solution)/shard_map/ppermute | solution.py:17
  50.0 5.9 %collective-permute-start.6 = (bf16[192,256]{1,0:T(8,128)(2,1)S(1)}, bf16[192,256]{1,0:T(8,128)(2,1)S(1)}, u32[]{:S(2)}, u32[]{:S(2)}) collective-permute-start(bf16[192,256]{1,0:T(8,128)(2,1)S(1)} %fusion.39), channel_id=1, source_target_pairs={{1,0},{2,1},{3,2},{4,3},{5,4},{6,5},{7,6},{8,7},{9,8},{10,9},{11,1... | collective-permute-start | bytes 294920 | tf_op jit(solution)/shard_map/ppermute | solution.py:17
  68.7 102.1 %reduce-scatter.7.cloned.1.call-start = ((), (), s32[]{:S(2)}) async-start(), calls=%async_computation.3 | async-start | bytes 786432 | tf_op jit(solution)/shard_map/reduce_scatter | solution.py:26
  256.3 20.8 %collective-permute-start.21 = (f32[16,256]{1,0:T(8,128)S(1)}, f32[16,256]{1,0:T(8,128)S(1)}, u32[]{:S(2)}, u32[]{:S(2)}) collective-permute-start(f32[16,256]{1,0:T(8,128)S(1)} %fusion), channel_id=1, source_target_pairs={{0,14},{1,15},{2,16},{3,17},{4,18},{5,19},{6,20},{7,21},{8,22},{9,... | collective-permute-start | bytes 49160
  260.9 29.8 %collective-permute-start.20 = (f32[16,256]{1,0:T(8,128)S(1)}, f32[16,256]{1,0:T(8,128)S(1)}, u32[]{:S(2)}, u32[]{:S(2)}) collective-permute-start(f32[16,256]{1,0:T(8,128)S(1)} %fusion), channel_id=1, source_target_pairs={{0,13},{1,14},{2,15},{3,16},{4,17},{5,18},{6,19},{7,20},{8,21},{9,... | collective-permute-start | bytes 49160
  265.3 27.1 %collective-permute-start.19 = (f32[16,256]{1,0:T(8,128)S(1)}, f32[16,256]{1,0:T(8,128)S(1)}, u32[]{:S(2)}, u32[]{:S(2)}) collective-permute-start(f32[16,256]{1,0:T(8,128)S(1)} %fusion), channel_id=1, source_target_pairs={{0,12},{1,13},{2,14},{3,15},{4,16},{5,17},{6,18},{7,19},{8,20},{9,... | collective-permute-start | bytes 49160
  266.6 27.4 %collective-permute-start.18 = (f32[16,256]{1,0:T(8,128)S(1)}, f32[16,256]{1,0:T(8,128)S(1)}, u32[]{:S(2)}, u32[]{:S(2)}) collective-permute-start(f32[16,256]{1,0:T(8,128)S(1)} %fusion), channel_id=1, source_target_pairs={{0,11},{1,12},{2,13},{3,14},{4,15},{5,16},{6,17},{7,18},{8,19},{9,... | collective-permute-start | bytes 49160
  267.9 6.2 %collective-permute-start.22 = (f32[11,256]{1,0:T(8,128)S(1)}, f32[11,256]{1,0:T(8,128)S(1)}, u32[]{:S(2)}, u32[]{:S(2)}) collective-permute-start(f32[11,256]{1,0:T(8,128)S(1)} %slice.51), channel_id=1, source_target_pairs={{0,15},{1,16},{2,17},{3,18},{4,19},{5,20},{6,21},{7,22},{8,23},{9,... | collective-permute-start | bytes 33800
  274.1 25.3 %collective-permute-start.17 = (f32[16,256]{1,0:T(8,128)S(1)}, f32[16,256]{1,0:T(8,128)S(1)}, u32[]{:S(2)}, u32[]{:S(2)}) collective-permute-start(f32[16,256]{1,0:T(8,128)S(1)} %fusion), channel_id=1, source_target_pairs={{0,10},{1,11},{2,12},{3,13},{4,14},{5,15},{6,16},{7,17},{8,18},{9,... | collective-permute-start | bytes 49160
  277.1 24.7 %collective-permute-start.16 = (f32[16,256]{1,0:T(8,128)S(1)}, f32[16,256]{1,0:T(8,128)S(1)}, u32[]{:S(2)}, u32[]{:S(2)}) collective-permute-start(f32[16,256]{1,0:T(8,128)S(1)} %fusion), channel_id=1, source_target_pairs={{0,9},{1,10},{2,11},{3,12},{4,13},{5,14},{6,15},{7,16},{8,17},{9,1... | collective-permute-start | bytes 49160
  290.7 14.0 %collective-permute-start.15 = (f32[16,256]{1,0:T(8,128)S(1)}, f32[16,256]{1,0:T(8,128)S(1)}, u32[]{:S(2)}, u32[]{:S(2)}) collective-permute-start(f32[16,256]{1,0:T(8,128)S(1)} %fusion), channel_id=1, source_target_pairs={{0,8},{1,9},{2,10},{3,11},{4,12},{5,13},{6,14},{7,15},{8,16},{9,17... | collective-permute-start | bytes 49160
  292.4 13.7 %collective-permute-start.14 = (f32[16,256]{1,0:T(8,128)S(1)}, f32[16,256]{1,0:T(8,128)S(1)}, u32[]{:S(2)}, u32[]{:S(2)}) collective-permute-start(f32[16,256]{1,0:T(8,128)S(1)} %fusion), channel_id=1, source_target_pairs={{0,7},{1,8},{2,9},{3,10},{4,11},{5,12},{6,13},{7,14},{8,15},{9,16}... | collective-permute-start | bytes 49160
  294.0 15.1 %collective-permute-start.13 = (f32[16,256]{1,0:T(8,128)S(1)}, f32[16,256]{1,0:T(8,128)S(1)}, u32[]{:S(2)}, u32[]{:S(2)}) collective-permute-start(f32[16,256]{1,0:T(8,128)S(1)} %fusion), channel_id=1, source_target_pairs={{0,6},{1,7},{2,8},{3,9},{4,10},{5,11},{6,12},{7,13},{8,14},{9,15},... | collective-permute-start | bytes 49160
  299.4 17.0 %collective-permute-start.12 = (f32[16,256]{1,0:T(8,128)S(1)}, f32[16,256]{1,0:T(8,128)S(1)}, u32[]{:S(2)}, u32[]{:S(2)}) collective-permute-start(f32[16,256]{1,0:T(8,128)S(1)} %fusion), channel_id=1, source_target_pairs={{0,5},{1,6},{2,7},{3,8},{4,9},{5,10},{6,11},{7,12},{8,13},{9,14},{... | collective-permute-start | bytes 49160
  301.8 14.6 %collective-permute-start.11 = (f32[16,256]{1,0:T(8,128)S(1)}, f32[16,256]{1,0:T(8,128)S(1)}, u32[]{:S(2)}, u32[]{:S(2)}) collective-permute-start(f32[16,256]{1,0:T(8,128)S(1)} %fusion), channel_id=1, source_target_pairs={{0,4},{1,5},{2,6},{3,7},{4,8},{5,9},{6,10},{7,11},{8,12},{9,13},{1... | collective-permute-start | bytes 49160
  304.7 11.8 %collective-permute-start.10 = (f32[16,256]{1,0:T(8,128)S(1)}, f32[16,256]{1,0:T(8,128)S(1)}, u32[]{:S(2)}, u32[]{:S(2)}) collective-permute-start(f32[16,256]{1,0:T(8,128)S(1)} %fusion), channel_id=1, source_target_pairs={{0,3},{1,4},{2,5},{3,6},{4,7},{5,8},{6,9},{7,10},{8,11},{9,12},{10... | collective-permute-start | bytes 49160
  306.0 10.4 %collective-permute-start.9 = (f32[16,256]{1,0:T(8,128)S(1)}, f32[16,256]{1,0:T(8,128)S(1)}, u32[]{:S(2)}, u32[]{:S(2)}) collective-permute-start(f32[16,256]{1,0:T(8,128)S(1)} %fusion), channel_id=1, source_target_pairs={{0,2},{1,3},{2,4},{3,5},{4,6},{5,7},{6,8},{7,9},{8,10},{9,11},{10,... | collective-permute-start | bytes 49160
  309.1 8.5 %collective-permute-start.8 = (f32[16,256]{1,0:T(8,128)S(1)}, f32[16,256]{1,0:T(8,128)}, u32[]{:S(2)}, u32[]{:S(2)}) collective-permute-start(f32[16,256]{1,0:T(8,128)S(1)} %fusion), channel_id=1, source_target_pairs={{0,1},{1,2},{2,3},{3,4},{4,5},{5,6},{6,7},{7,8},{8,9},{9,10},{10,1... | collective-permute-start | bytes 49160
  (15 other events, 147.3 us)
Sparse Core Ops, SparseCore 0:
  68.8 73.0 reduce-scatter.4
  145.0 25.7 reduce-scatter.6
where the time goes:
time: 388 us; the launch traced here: 386 us
  blocking collectives  135 us (35%)
  waiting for transfers between devices  121 us (31%)
  starting transfers between devices  74.4 us (19%)
  local copies, waits for them, and re-layouts  26 us (7%)
  between operations  15.3 us (4%)
  matrix products  11.7 us (3%)
    reduce_scatter x2, waiting for transfers between devices, sum_in_order(): parts = lax.psum_scatter(parts, axes[k], scatter_dimension=0, tiled=True)  102 us
    unnamed x1, blocking collectives  83.7 us
    unnamed x15, starting transfers between devices  53.2 us
    all_gather x1, blocking collectives, total_of(): whole = lax.all_gather(own, axis).reshape(-1, *lines.shape[1:])  51.2 us
    ppermute x8, starting transfers between devices, shifted(): lax.ppermute(value, axis, [(source, source + steps) for source in range(f...  21.2 us
    ppermute x8, waiting for transfers between devices, shifted(): lax.ppermute(value, axis, [(source, source + steps) for source in range(f...  18.5 us
    unnamed x38, local copies, waits for them, and re-layouts  15.7 us
  transfers between devices with their start and end apart: 25, of which 9 were waited for; matrix products, arithmetic and copies ran while one was open for 2% of the time, Pallas kernels for 0%

commit v1 on v0

v1 whole, which is shorter than its diff:
```python
import functools

import jax
import jax.numpy as jnp
from jax import lax
from jax.experimental import pallas as pl
from jax.experimental.pallas import tpu as pltpu
from jax.sharding import Mesh
from jax.sharding import PartitionSpec as P

HD = 128
HQ = 8
WIN = 3
AXES = ("x_hi", "y", "z", "x_lo", "core")
MESH = pl.DeviceIdType.MESH
BF16 = jnp.bfloat16
F32 = jnp.float32
NT = (((1,), (1,)), ((), ()))


def dot(a, b):
    return jnp.dot(a, b, preferred_element_type=F32)


def dot_nt(a, b):
    return lax.dot_general(a, b, NT, preferred_element_type=F32)


def kernel(
    ny, nz, tok, chunk,
    x_hbm, q_hbm, kv_hbm, do_hbm, lse_hbm, delta_hbm,
    dq_out, gkv_out, gw_out,
    qs, dos, lse_in, delta_in, rows, kvb, ds_all, gsend, grecv, xa, xb, g6, gt,
    keep, xs, xr, ys, yr, zsrc, zr, za, fin,
    load_sem, xl_sem, kv_send, kv_recv, gr_send, gr_recv, xsnd, xrcv, g_send, g_recv,
    xs_send, xs_recv, y_send, y_recv, zr_send, zr_recv, za_send, za_recv, f_send, f_recv,
):
    h = lax.axis_index("x_hi")
    y = lax.axis_index("y")
    z = lax.axis_index("z")
    l = lax.axis_index("x_lo")
    c = lax.axis_index("core")
    n_inner = nz * 4
    inner = z * 4 + l * 2 + c
    n_outer = 2 * ny
    outer = h * ny + y
    scaling = HD ** (-0.5)

    def inner_dev(step):
        j = lax.rem(inner + step + n_inner, n_inner)
        return {"z": j // 4, "x_lo": lax.rem(j // 2, 2), "core": lax.rem(j, 2)}

    def outer_dev(step):
        j = lax.rem(outer + step + n_outer, n_outer)
        return {"x_hi": j // ny, "y": lax.rem(j, ny)}

    core_dev = {"core": 1 - c}
    p1_same = {"x_lo": 1 - l}
    p1_other = {"x_lo": 1 - l, "core": 1 - c}
    p2_same = {"x_hi": 1 - h, "x_lo": 1 - l}
    p2_other = {"x_hi": 1 - h, "x_lo": 1 - l, "core": 1 - c}

    def y_dev(d):
        return {"y": lax.rem(y + d, ny)}

    def z_dev(d):
        return {"z": lax.rem(z + d, nz)}

    def remote(src, dst, send, recv, device):
        return pltpu.make_async_remote_copy(
            src_ref=src, dst_ref=dst, send_sem=send, recv_sem=recv, device_id=device, device_id_type=MESH
        )

    loads = []
    for k in range(HQ):
        part, cols = pl.ds(k * tok, tok), pl.ds(k * HD, HD)
        loads.append(pltpu.make_async_copy(q_hbm.at[:, cols], qs.at[part, :], load_sem.at[k]))
        loads.append(pltpu.make_async_copy(do_hbm.at[:, cols], dos.at[part, :], load_sem.at[HQ + k]))
    loads.append(pltpu.make_async_copy(lse_hbm, lse_in, load_sem.at[2 * HQ]))
    loads.append(pltpu.make_async_copy(delta_hbm, delta_in, load_sem.at[2 * HQ + 1]))
    loads.append(pltpu.make_async_copy(kv_hbm, kvb.at[0], load_sem.at[2 * HQ + 2]))
    for copy in loads:
        copy.start()

    greeted = [inner_dev(s) for s in (1, 2, 3, -1, -2, -3)] + [outer_dev(1), outer_dev(-1)]
    greeted += [core_dev, p1_same, p1_other, p2_same, p2_other]
    greeted += [y_dev(d) for d in range(1, ny)] + [z_dev(d) for d in range(1, nz)]
    barrier = pltpu.get_barrier_semaphore()
    for device in greeted:
        pl.semaphore_signal(barrier, inc=1, device_id=device, device_id_type=MESH)
    pl.semaphore_wait(barrier, len(greeted))

    kv_copies = []
    for w in range(1, WIN + 2):
        device = inner_dev(w) if w <= WIN else outer_dev(1)
        kv_copies.append(remote(kv_hbm, kvb.at[w], kv_send.at[w - 1], kv_recv.at[w - 1], device))
        kv_copies[-1].start()

    half = ny // 2
    shard = 512

    def columns(hh, ll, cc, d):
        yy = lax.rem(y + d, ny)
        return pl.ds(pl.multiple_of((hh * ny + yy) * shard + (cc * 2 + ll) * 128, 128), 128)

    def send_columns(k, carry):
        d_a, d_b = half + k, half - 1 - k

        def slot(s):
            return pl.ds(pl.multiple_of(k * 256 + s * 128, 128), 128)

        for s in range(2):
            def from_a(hh, ll, cc):
                return x_hbm.at[:, columns(1 - hh if s else hh, 1 - ll if s else ll, cc, d_a)]

            def from_b(hh, ll, cc):
                return x_hbm.at[:, columns(hh, 1 - ll if s else ll, cc, d_b)]

            pltpu.make_async_copy(from_a(h, l, c), xa.at[pl.ds(2 * tok, tok), slot(s)], xl_sem.at[0]).start()
            pltpu.make_async_copy(from_b(h, l, c), xb.at[pl.ds(0, tok), slot(s)], xl_sem.at[1]).start()
            remote(from_a(h, 1 - l, c), xa.at[pl.ds(0, tok), slot(s)], xsnd.at[0], xrcv.at[0], p1_same).start()
            remote(
                from_b(1 - h, 1 - l, c), xb.at[pl.ds(2 * tok, tok), slot(s)], xsnd.at[1], xrcv.at[1], p2_same
            ).start()
            remote(
                from_a(h, 1 - l, 1 - c), xa.at[pl.ds(tok, tok), slot(s)], xsnd.at[2], xrcv.at[2], p1_other
            ).start()
            remote(
                from_b(1 - h, 1 - l, 1 - c), xb.at[pl.ds(3 * tok, tok), slot(s)], xsnd.at[3], xrcv.at[3], p2_other
            ).start()
            remote(
                from_a(h, l, 1 - c), xa.at[pl.ds(3 * tok, tok), slot(s)], xsnd.at[4], xrcv.at[4], core_dev
            ).start()
            remote(from_b(h, l, 1 - c), xb.at[pl.ds(tok, tok), slot(s)], xsnd.at[5], xrcv.at[5], core_dev).start()
        return carry

    lax.fori_loop(0, half, send_columns, 0)
    x_places = [
        (xa, 0, p1_same), (xb, 2, p2_same), (xa, 1, p1_other), (xb, 3, p2_other), (xa, 3, core_dev), (xb, 1, core_dev)
    ]
    x_copies = []
    for k, (buffer, place, device) in enumerate(x_places):
        whole = buffer.at[pl.ds(place * tok, tok), :]
        x_copies.append(remote(whole, whole, xsnd.at[k], xrcv.at[k], device))

    for copy in loads:
        copy.wait()
    for k in range(HQ):
        rows[0:1, k * tok : (k + 1) * tok] = lse_in[k : k + 1, :]
        rows[8:9, k * tok : (k + 1) * tok] = delta_in[k : k + 1, :]

    wide = 2 * tok
    key_pos = lax.broadcasted_iota(jnp.int32, (tok, wide), 0)
    lane = lax.broadcasted_iota(jnp.int32, (tok, wide), 1)
    query_pos = jnp.where(lane >= tok, lane - tok, lane)
    causal = key_pos <= query_pos

    def attend(w):
        key = kvb[w, :, :HD]
        value = kvb[w, :, HD:]
        if w == 0:
            penalty = None
        elif w <= WIN:
            penalty = jnp.where(inner >= w, 0.0, 1e30).astype(F32)
        else:
            penalty = jnp.where(outer >= 1, 0.0, 1e30).astype(F32)
        grad_key = jnp.zeros((tok, HD), F32)
        grad_value = jnp.zeros((tok, HD), F32)
        for k in range(HQ // 2):
            part = slice(k * wide, (k + 1) * wide)
            query, cotangent = qs[part, :], dos[part, :]
            lse, delta = rows[0:1, part], rows[8:9, part]
            if penalty is not None:
                lse = lse + penalty
            scores = dot_nt(key, query) * scaling - lse
            if penalty is None:
                scores = jnp.where(causal, scores, -1e30)
            probs = jnp.exp(scores)
            grad_probs = dot_nt(value, cotangent)
            grad_scores = (probs * (grad_probs - delta) * scaling).astype(BF16)
            ds_all[w * tok : (w + 1) * tok, part] = grad_scores
            grad_key = grad_key + dot(grad_scores, query)
            grad_value = grad_value + dot(probs.astype(BF16), cotangent)
        return grad_key, grad_value

    own_key, own_value = attend(0)
    grad_copies = {}
    for w in (3, 4, 2, 1):
        kv_copies[w - 1].wait_recv()
        grad_key, grad_value = attend(w)
        gsend[w - 1, :, :HD] = grad_key.astype(BF16)
        gsend[w - 1, :, HD:] = grad_value.astype(BF16)
        device = inner_dev(-w) if w <= WIN else outer_dev(-1)
        grad_copies[w] = remote(
            gsend.at[w - 1], grecv.at[w - 1], gr_send.at[w - 1], gr_recv.at[w - 1], device
        )
        grad_copies[w].start()

    keys_all = jnp.concatenate([kvb[w, :, :HD] for w in range(WIN + 2)], axis=0)
    keys_t = keys_all.T
    for k in range(HQ // 2):
        part = slice(k * wide, (k + 1) * wide)
        turned = dot(keys_t, ds_all[:, part]).T.astype(BF16)
        dq_out[:, 2 * k * HD : (2 * k + 1) * HD] = turned[:tok]
        dq_out[:, (2 * k + 1) * HD : (2 * k + 2) * HD] = turned[tok:]

    for w in (3, 4, 2, 1):
        grad_copies[w].wait_recv()
        own_key = own_key + grecv[w - 1, :, :HD].astype(F32)
        own_value = own_value + grecv[w - 1, :, HD:].astype(F32)
    grad_kv = jnp.concatenate([own_key, own_value], axis=1).astype(BF16)
    own_rows = pl.ds(2 * tok, tok)
    g6[own_rows, :] = grad_kv
    gkv_out[...] = grad_kv

    g_copies = []
    for k, (place, device) in enumerate(
        ((3, core_dev), (0, p1_same), (4, p2_same), (1, p1_other), (5, p2_other))
    ):
        g_copies.append(
            remote(g6.at[own_rows, :], g6.at[pl.ds(place * tok, tok), :], g_send.at[k], g_recv.at[k], device)
        )
        g_copies[-1].start()

    def turn(pair):
        gt[:, pair * wide : (pair + 1) * wide] = g6[pair * wide : (pair + 1) * wide, :].T

    own_a = xa.at[pl.ds(2 * tok, tok), :]
    own_b = xb.at[pl.ds(0, tok), :]
    pltpu.make_async_copy(own_a, own_a, xl_sem.at[0]).wait()
    pltpu.make_async_copy(own_b, own_b, xl_sem.at[1]).wait()
    g_copies[0].wait_recv()
    turn(1)
    for k in (1, 3):
        g_copies[k].wait_recv()
    turn(0)
    for k in (2, 4):
        g_copies[k].wait_recv()
    turn(2)
    for copy in x_copies:
        copy.wait_recv()

    order = []
    for k in range(half):
        order += [half + k, half - 1 - k]
    x_sums = {}
    for d in order:
        if d >= half:
            k = d - half
            product = dot(gt[:, : 4 * tok], xa[:, k * 256 : (k + 1) * 256])
        else:
            k = half - 1 - d
            product = dot(gt[:, 2 * tok :], xb[:, k * 256 : (k + 1) * 256])
        keep[d] = product[:, :128]
        xs[d] = product[:, 128:].astype(BF16)
        x_sums[d] = remote(
            xs.at[d], xr.at[d], xs_send.at[d], xs_recv.at[d], p2_same if d >= half else p1_same
        )
        x_sums[d].start()

    y_sums = {}
    for d in order:
        x_sums[d].wait_recv()
        total = keep[d] + xr[d].astype(F32)
        if d == 0:
            own_total = total
        else:
            ys[d] = total.astype(BF16)
            y_sums[d] = remote(ys.at[d], yr.at[d], y_send.at[d], y_recv.at[d], y_dev(d))
            y_sums[d].start()
    for d in order:
        if d != 0:
            y_sums[d].wait_recv()
            own_total = own_total + yr[d].astype(F32)

    zsrc[0:256, :] = own_total
    if chunk * nz > 256:
        zsrc[256:, :] = jnp.zeros((chunk * nz - 256, 128), F32)
    z_order = sorted(range(1, nz), key=lambda d: -min(d, nz - d))
    z_sums = {}
    for d in z_order:
        there = lax.rem(z + d, nz)
        z_sums[d] = remote(
            zsrc.at[pl.ds(pl.multiple_of(there * chunk, 8), chunk), :], zr.at[d], zr_send.at[d], zr_recv.at[d], z_dev(d)
        )
        z_sums[d].start()
    here = pl.ds(pl.multiple_of(z * chunk, 8), chunk)
    piece = zsrc[here, :]
    for d in reversed(z_order):
        z_sums[d].wait_recv()
        piece = piece + zr[d]
    za[here, :] = piece
    z_all = {}
    for d in z_order:
        z_all[d] = remote(za.at[here, :], za.at[here, :], za_send.at[d], za_recv.at[d], z_dev(d))
        z_all[d].start()
    for d in reversed(z_order):
        z_all[d].wait_recv()

    quarter = c * 2 + l
    place = pl.ds(pl.multiple_of(quarter * 128, 128), 128)
    fin[place, :] = za[0:256, :].T.astype(BF16)
    ends = []
    for k, device in enumerate((p1_same, p1_other, core_dev)):
        ends.append(remote(fin.at[place, :], fin.at[place, :], f_send.at[k], f_recv.at[k], device))
        ends[-1].start()
    for copy in ends:
        copy.wait_recv()
    gw_out[...] = fin[...]

    for copy in kv_copies + list(grad_copies.values()) + x_copies + g_copies + list(x_sums.values()):
        copy.wait_send()
    for copy in list(y_sums.values()) + list(z_sums.values()) + list(z_all.values()) + ends:
        copy.wait_send()


def local(ny, nz, layer_input, query, keys_values, grad_output, logsumexp, delta):
    tok = query.shape[0]
    heads = HQ * tok
    chunk = -(-32 // nz) * 8
    dma = pltpu.SemaphoreType.DMA
    half = ny // 2
    any_spec = pl.BlockSpec(memory_space=pl.ANY)
    vmem_spec = pl.BlockSpec(memory_space=pltpu.VMEM)
    grad_query, grad_kv, grad_weight = pl.pallas_call(
        functools.partial(kernel, ny, nz, tok, chunk),
        out_shape=(
            jax.ShapeDtypeStruct((tok, HQ * HD), BF16),
            jax.ShapeDtypeStruct((tok, 2 * HD), BF16),
            jax.ShapeDtypeStruct((512, 2 * HD), BF16),
        ),
        in_specs=[any_spec] * 6,
        out_specs=(vmem_spec, vmem_spec, vmem_spec),
        scratch_shapes=[
            pltpu.VMEM((heads, HD), BF16),
            pltpu.VMEM((heads, HD), BF16),
            pltpu.VMEM((HQ, tok), F32),
            pltpu.VMEM((HQ, tok), F32),
            pltpu.VMEM((16, heads), F32),
            pltpu.VMEM((WIN + 2, tok, 2 * HD), BF16),
            pltpu.VMEM(((WIN + 2) * tok, heads), BF16),
            pltpu.VMEM((WIN + 1, tok, 2 * HD), BF16),
            pltpu.VMEM((WIN + 1, tok, 2 * HD), BF16),
            pltpu.VMEM((4 * tok, half * 256), BF16),
            pltpu.VMEM((4 * tok, half * 256), BF16),
            pltpu.VMEM((6 * tok, 2 * HD), BF16),
            pltpu.VMEM((2 * HD, 6 * tok), BF16),
            pltpu.VMEM((ny, 256, 128), F32),
            pltpu.VMEM((ny, 256, 128), BF16),
            pltpu.VMEM((ny, 256, 128), BF16),
            pltpu.VMEM((ny, 256, 128), BF16),
            pltpu.VMEM((ny, 256, 128), BF16),
            pltpu.VMEM((chunk * nz, 128), F32),
            pltpu.VMEM((nz, chunk, 128), F32),
            pltpu.VMEM((chunk * nz, 128), F32),
            pltpu.VMEM((512, 2 * HD), BF16),
            dma((2 * HQ + 3,)),
            dma((2,)),
            dma((WIN + 1,)),
            dma((WIN + 1,)),
            dma((WIN + 1,)),
            dma((WIN + 1,)),
            dma((6,)),
            dma((6,)),
            dma((5,)),
            dma((5,)),
            dma((ny,)),
            dma((ny,)),
            dma((ny,)),
            dma((ny,)),
            dma((nz,)),
            dma((nz,)),
            dma((nz,)),
            dma((nz,)),
            dma((3,)),
            dma((3,)),
        ],
        compiler_params=pltpu.CompilerParams(
            collective_id=0, has_side_effects=True, vmem_limit_bytes=56 * 1024 * 1024
        ),
    )(layer_input, query, keys_values, grad_output, logsumexp.T, delta.T)
    return grad_query, grad_kv, grad_weight.astype(F32)


def solution(mesh):
    ny = mesh.shape["outer"] // 2
    nz = mesh.shape["inner"] // 4
    finer = Mesh(mesh.devices.reshape(2, ny, nz, 2, 2), AXES)
    tokens = P(AXES, None)
    return jax.shard_map(
        functools.partial(local, ny, nz),
        mesh=finer,
        in_specs=(tokens,) * 6,
        out_specs=(tokens, tokens, P(("x_hi", "y"), None)),
        check_vma=False,
    )
```

time: 388 us -> 96.3 us (0.25)
  blocking collectives: 135 us -> 0 us
  waiting for transfers between devices: 121 us -> 0 us
  Pallas kernels: 0 us -> 90.4 us
  starting transfers between devices: 74.4 us -> 0 us
  local copies, waits for them, and re-layouts: 26 us -> 3.3 us
  between operations: 15.3 us -> 0.64 us
  matrix products: 11.7 us -> 0 us
    reduce_scatter x2 -> x0, waiting for transfers between devices: 102 us -> none  [sum_in_order(): parts = lax.psum_scatter(parts, axes[k], scatter_dimension=0, tiled=True)]
    pallas_call x0 -> x1, Pallas kernels: none -> 90.4 us  [local(): pl.pallas_call(functools.partial(kernel, ny, nz, tok, chunk), out_shape=(...]
    unnamed x1 -> x0, blocking collectives: 83.7 us -> none
    unnamed x15 -> x0, starting transfers between devices: 53.2 us -> none
    all_gather x1 -> x0, blocking collectives: 51.2 us -> none  [total_of(): whole = lax.all_gather(own, axis).reshape(-1, *lines.shape[1:])]
    ppermute x8 -> x0, starting transfers between devices: 21.2 us -> none  [shifted(): lax.ppermute(value, axis, [(source, source + steps) for source in range(f...]
    ppermute x8 -> x0, waiting for transfers between devices: 18.5 us -> none  [shifted(): lax.ppermute(value, axis, [(source, source + steps) for source in range(f...]
    unnamed x38 -> x2, local copies, waits for them, and re-layouts: 15.7 us -> 3.3 us
  transfers between devices with their start and end apart: 25 -> 0, of which waited for: 9 -> 0; matrix products, arithmetic and copies ran while one was open for 2% -> 0% of each run, Pallas kernels for 0% -> 0%
where the time goes in v1:
time: 96.3 us; the launch traced here: 96.1 us
  Pallas kernels  90.4 us (94%)
  local copies, waits for them, and re-layouts  3.3 us (3%)
  other arithmetic  1.78 us (2%)
    pallas_call x1, Pallas kernels, local(): pl.pallas_call(functools.partial(kernel, ny, nz, tok, chunk), out_shape=(...  90.4 us
    unnamed x2, local copies, waits for them, and re-layouts  3.3 us

profile of v1, /device:TPU:1, one launch (start us, length us, event | category | flops | bytes accessed | tf_op | source)
XLA Modules:
  0.0 96.1 jit_solution(16220761648131167189)
XLA Ops:
  0.6 90.4 %shard_map.85 = (bf16[192,1024]{1,0:T(8,128)(2,1)}, bf16[192,256]{1,0:T(8,128)(2,1)}, bf16[512,256]{1,0:T(8,128)(2,1)}) custom-call(bf16[192,8192]{1,0:T(8,128)(2,1)} %x_hbm.1, bf16[192,1024]{1,0:T(8,128)(2,1)} %q_hbm.1, bf16[192,256]{1,0:T(8,128)(2,1)} %kv_hbm.1, bf16[192,1024]{1,0:T(8,128)(2,1)} %do_hbm.1, f32[8,192]{1,0:T(8,128)} %bitcast.2, f32[8,192]{1,0:T(8,128)} %bitcast.3), custom_call_target="tpu_custom_call" | custom-call | tf_op jit(solution)/shard_map/pallas_call | solution.py:325
  91.0 1.8 %convert_element_type.3 = f32[512,256]{1,0:T(8,128)} convert(bf16[512,256]{1,0:T(8,128)(2,1)} %get-tuple-element.8) | non-fusion elementwise | flops 131072 | bytes 786432 | tf_op jit(solution)/shard_map/convert_element_type | solution.py:382
  92.8 1.8 %copy.11 = bf16[192,1024]{1,0:T(8,128)(2,1)} copy(bf16[192,1024]{1,0:T(8,128)(2,1)} %get-tuple-element.12) | data formatting | bytes 786432
  94.6 1.5 %copy.12 = bf16[192,256]{1,0:T(8,128)(2,1)} copy(bf16[192,256]{1,0:T(8,128)(2,1)} %get-tuple-element.13) | data formatting | bytes 196608

commit v2 on v1

v2 whole, which is shorter than its diff:
```python
import functools

import jax
import jax.numpy as jnp
from jax import lax
from jax.experimental import pallas as pl
from jax.experimental.pallas import tpu as pltpu
from jax.sharding import Mesh
from jax.sharding import PartitionSpec as P

HD = 128
HQ = 8
WIN = 3
AXES = ("x_hi", "y", "z", "x_lo", "core")
MESH = pl.DeviceIdType.MESH
BF16 = jnp.bfloat16
F32 = jnp.float32
NT = (((1,), (1,)), ((), ()))
LOG2E = 1.4426950408889634


def dot(a, b):
    return jnp.dot(a, b, preferred_element_type=F32)


def dot_nt(a, b):
    return lax.dot_general(a, b, NT, preferred_element_type=F32)


def kernel(
    ny, nz, tok, lists, owners,
    x_hbm, q_hbm, kv_hbm, do_hbm, lse_hbm, delta_hbm,
    dq_out, gkv_out, gw_out,
    qs, dos, lse_in, delta_in, rows, kvb, ds_all, gsend, grecv, x_own, x_pair, gs, gt,
    keep, xs, xr, ys, yr, zsrc, zr, fin,
    load_sem, x_local, kv_send, kv_recv, gr_send, gr_recv, xsnd, xrcv, g_send, g_recv,
    xs_send, xs_recv, y_send, y_recv, zr_send, zr_recv, za_send, za_recv, f_send, f_recv,
):
    h = lax.axis_index("x_hi")
    y = lax.axis_index("y")
    z = lax.axis_index("z")
    l = lax.axis_index("x_lo")
    c = lax.axis_index("core")
    n_inner = nz * 4
    inner = z * 4 + l * 2 + c
    n_outer = 2 * ny
    outer = h * ny + y
    scaling = HD ** (-0.5)

    def inner_dev(step):
        j = lax.rem(inner + step + n_inner, n_inner)
        return {"z": j // 4, "x_lo": lax.rem(j // 2, 2), "core": lax.rem(j, 2)}

    def outer_dev(step):
        j = lax.rem(outer + step + n_outer, n_outer)
        return {"x_hi": j // ny, "y": lax.rem(j, ny)}

    z_m = lax.rem(z + 1 - 2 * l + nz, nz)
    z_n = lax.rem(z - 1 + 2 * l + nz, nz)
    core_dev = {"core": 1 - c}
    p1_same = {"x_lo": 1 - l}
    p1_other = {"x_lo": 1 - l, "core": 1 - c}
    p2_same = {"x_hi": 1 - h, "x_lo": 1 - l}
    p2_other = {"x_hi": 1 - h, "x_lo": 1 - l, "core": 1 - c}
    zm_same, zm_other = {"z": z_m}, {"z": z_m, "core": 1 - c}
    zn_same, zn_other = {"z": z_n}, {"z": z_n, "core": 1 - c}

    def y_dev(d):
        return {"y": lax.rem(y + d, ny)}

    def z_dev(d):
        return {"z": lax.rem(z + d, nz)}

    def remote(src, dst, send, recv, device):
        return pltpu.make_async_remote_copy(
            src_ref=src, dst_ref=dst, send_sem=send, recv_sem=recv, device_id=device, device_id_type=MESH
        )

    z_order = sorted(range(1, nz), key=lambda d: -min(d, nz - d))
    y_order = sorted(range(1, ny), key=lambda d: -min(d, ny - d))

    loads = []
    for k in range(HQ):
        part, cols = pl.ds(k * tok, tok), pl.ds(k * HD, HD)
        pltpu.make_async_copy(q_hbm.at[:, cols], qs.at[part, :], load_sem.at[0]).start()
        pltpu.make_async_copy(do_hbm.at[:, cols], dos.at[part, :], load_sem.at[1]).start()
    loads.append(pltpu.make_async_copy(lse_hbm, lse_in, load_sem.at[2]))
    loads.append(pltpu.make_async_copy(delta_hbm, delta_in, load_sem.at[3]))
    loads.append(pltpu.make_async_copy(kv_hbm, kvb.at[0], load_sem.at[4]))
    for copy in loads:
        copy.start()
    loads.append(pltpu.make_async_copy(qs, qs, load_sem.at[0]))
    loads.append(pltpu.make_async_copy(dos, dos, load_sem.at[1]))

    with jax.named_scope("greet"):
        greeted = [z_dev(d) for d in z_order] + [y_dev(d) for d in y_order] + [outer_dev(1), outer_dev(-1)]
        greeted += [inner_dev(6 * c - 3), inner_dev(2), inner_dev(-2)]
        greeted += [p1_other, p2_other, zm_other, zn_other, p1_same, p2_same, core_dev]
        barrier = pltpu.get_barrier_semaphore()
        for device in greeted:
            pl.semaphore_signal(barrier, inc=1, device_id=device, device_id_type=MESH)
        pl.semaphore_wait(barrier, len(greeted))

    before = (0, 2, 1 + 2 * c, 3 - 2 * c)
    kv_copies = {}
    for slot, device in ((1, inner_dev(2)), (3, inner_dev(1 + 2 * c)), (4, outer_dev(1))):
        kv_copies[slot] = remote(kv_hbm, kvb.at[slot], kv_send.at[slot - 1], kv_recv.at[slot - 1], device)
        kv_copies[slot].start()

    far = 1 - lax.rem(l + z, 2)
    steps_a, steps_b, steps_c, steps_e = lists
    size = len(steps_a)
    distances = [
        list(steps_a),
        list(steps_b),
        [e + far * (s - e) for s, e in zip(steps_c, steps_e)],
        [s + far * (e - s) for s, e in zip(steps_c, steps_e)],
    ]
    def places(which, hh, ll):
        return (
            ((hh, ll), (1 - hh, 1 - ll)),
            ((hh, ll), (hh, 1 - ll)),
            ((hh, ll), (1 - hh, ll)),
            ((hh, 1 - ll), (1 - hh, 1 - ll)),
        )[which]

    shard = 512
    pairs = (
        (0, 0, (h, 1 - l), p1_same, p1_other),
        (1, 1, (1 - h, 1 - l), p2_same, p2_other),
        (2, 3, (h, l), zm_same, zm_other),
        (3, 2, (h, l), zn_same, zn_other),
    )
    with jax.named_scope("issue_columns"):
        for k in range(size):
            for s in range(2):
                slot = pl.ds(k * 256 + s * 128, 128)
                for mine, theirs, (hh, ll), same, other in pairs:
                    shards = lax.rem(y + distances[mine][k], ny) * shard

                    def columns(place, cc):
                        start = place[0] * (ny * shard) + shards + (cc * 2 + place[1]) * 128
                        return x_hbm.at[:, pl.ds(pl.multiple_of(start, 128), 128)]

                    there = places(theirs, hh, ll)[s]
                    here = places(mine, h, l)[s]
                    remote(
                        columns(there, c), x_pair.at[theirs, pl.ds(0, tok), slot],
                        xsnd.at[0], xrcv.at[theirs], same,
                    ).start()
                    remote(
                        columns(there, 1 - c), x_pair.at[theirs, pl.ds(tok, tok), slot],
                        xsnd.at[1], xrcv.at[theirs], other,
                    ).start()
                    remote(
                        columns(here, 1 - c), x_own.at[mine, pl.ds(tok, tok), slot],
                        xsnd.at[2], xrcv.at[4], core_dev,
                    ).start()
                    pltpu.make_async_copy(
                        columns(here, c), x_own.at[mine, pl.ds(0, tok), slot], x_local.at[0]
                    ).start()
    from_own = x_own.at[:, pl.ds(0, tok), :]
    from_core = x_own.at[:, pl.ds(tok, tok), :]
    from_same = x_pair.at[:, pl.ds(0, tok), :]
    from_other = x_pair.at[:, pl.ds(tok, tok), :]

    with jax.named_scope("load_wait"):
        for copy in loads:
            copy.wait()
    for k in range(HQ):
        rows[0:1, k * tok : (k + 1) * tok] = lse_in[k : k + 1, :] * LOG2E
        rows[8:9, k * tok : (k + 1) * tok] = delta_in[k : k + 1, :]

    wide = 2 * tok
    heads = HQ // 2
    key_pos = lax.broadcasted_iota(jnp.int32, (tok, heads * tok), 0)
    lane = lax.broadcasted_iota(jnp.int32, (tok, heads * tok), 1)
    causal = key_pos <= lax.rem(lane, tok)

    def attend(w):
        key = kvb[w, :, :HD]
        value = kvb[w, :, HD:]
        if w == 0:
            penalty = None
        elif w <= WIN:
            penalty = jnp.where(inner >= before[w], 0.0, 1e30).astype(F32)
        else:
            penalty = jnp.where(outer >= 1, 0.0, 1e30).astype(F32)
        grad_key = jnp.zeros((tok, HD), F32)
        grad_value = jnp.zeros((tok, HD), F32)
        for k in range(HQ // heads):
            part = slice(k * heads * tok, (k + 1) * heads * tok)
            query, cotangent = qs[part, :], dos[part, :]
            lse, delta = rows[0:1, part], rows[8:9, part]
            if penalty is not None:
                lse = lse + penalty
            scores = dot_nt(key, query) * (scaling * LOG2E) - lse
            if penalty is None:
                scores = jnp.where(causal, scores, -1e30)
            probs = jnp.exp2(scores)
            grad_probs = dot_nt(value, cotangent)
            grad_scores = (probs * (grad_probs - delta) * scaling).astype(BF16)
            ds_all[w * tok : (w + 1) * tok, part] = grad_scores
            grad_key = grad_key + dot(grad_scores, query)
            grad_value = grad_value + dot(probs.astype(BF16), cotangent)
        return grad_key, grad_value

    with jax.named_scope("own_block"):
        own_key, own_value = attend(0)
    with jax.named_scope("kv_wait"):
        kv_copies[1].wait_recv()
        kv_copies[2] = remote(kvb.at[1], kvb.at[2], kv_send.at[1], kv_recv.at[1], core_dev)
        kv_copies[2].start()
    grad_copies = {}
    for w, device in ((3, inner_dev(2 * c - 3)), (4, outer_dev(-1)), (2, core_dev), (1, inner_dev(-2))):
        if w != 1:
            with jax.named_scope("kv_wait"):
                kv_copies[w].wait_recv()
        with jax.named_scope("attend"):
            grad_key, grad_value = attend(w)
        if w == 1:
            with jax.named_scope("merge_wait"):
                grad_copies[2].wait_recv()
            grad_key = grad_key + grecv[1, :, :HD].astype(F32)
            grad_value = grad_value + grecv[1, :, HD:].astype(F32)
        gsend[w - 1, :, :HD] = grad_key.astype(BF16)
        gsend[w - 1, :, HD:] = grad_value.astype(BF16)
        grad_copies[w] = remote(
            gsend.at[w - 1], grecv.at[w - 1], gr_send.at[w - 1], gr_recv.at[w - 1], device
        )
        grad_copies[w].start()

    with jax.named_scope("grad_query"):
        keys_t = jnp.concatenate([kvb[w, :, :HD] for w in range(WIN + 2)], axis=0).T
        for k in range(HQ // 2):
            part = slice(k * wide, (k + 1) * wide)
            turned = dot(keys_t, ds_all[:, part]).T.astype(BF16)
            dq_out[:, 2 * k * HD : (2 * k + 1) * HD] = turned[:tok]
            dq_out[:, (2 * k + 1) * HD : (2 * k + 2) * HD] = turned[tok:]

    with jax.named_scope("grads_wait"):
        for w in (3, 4, 1):
            grad_copies[w].wait_recv()
            own_key = own_key + grecv[w - 1, :, :HD].astype(F32)
            own_value = own_value + grecv[w - 1, :, HD:].astype(F32)
    grad_kv = jnp.concatenate([own_key, own_value], axis=1).astype(BF16)
    gs[0:tok, :] = grad_kv

    g_copies = {}
    for place, device in ((2, p1_same), (4, p2_same), (8, zm_same), (6, zn_same), (1, core_dev)):
        g_copies[place] = remote(
            gs.at[pl.ds(0, tok), :], gs.at[pl.ds(place * tok, tok), :], g_send.at[0], g_recv.at[place], device
        )
        g_copies[place].start()
    gkv_out[...] = grad_kv

    def turn(pair):
        gt[:, pair * wide : (pair + 1) * wide] = gs[pair * wide : (pair + 1) * wide, :].T

    x_sums = {}

    def push(slot, value, device):
        xs[slot] = value.astype(BF16)
        x_sums[slot] = remote(xs.at[slot], xr.at[slot], xs_send.at[0], xs_recv.at[slot], device)
        x_sums[slot].start()

    with jax.named_scope("core_wait"):
        pltpu.make_async_copy(from_own, from_own, x_local.at[0]).wait()
        remote(from_core, from_core, xsnd.at[2], xrcv.at[4], core_dev).wait_recv()
        g_copies[1].wait_recv()
        turn(0)
    with jax.named_scope("pass_on"):
        for place in (6, 2, 4, 8):
            g_copies[place].wait_recv()
            g_copies[place + 1] = remote(
                gs.at[pl.ds(place * tok, tok), :], gs.at[pl.ds((place + 1) * tok, tok), :],
                g_send.at[0], g_recv.at[place + 1], core_dev,
            )
            g_copies[place + 1].start()

    for mine in (2, 0, 1, 3):
        with jax.named_scope("pair_wait"):
            place = {0: 2, 1: 4, 2: 6, 3: 8}[mine]
            g_copies[place + 1].wait_recv()
            turn(place // 2)
            remote(x_pair.at[mine], x_pair.at[mine], xsnd.at[0], xrcv.at[mine], pairs[mine][3]).wait_recv()
        with jax.named_scope("multiply"):
            for k in range(size):
                cols = slice(k * 256, (k + 1) * 256)
                product = dot(gt[:, :wide], x_own[mine, :, cols])
                product = product + dot(gt[:, place * tok : (place + 2) * tok], x_pair[mine, :, cols])
                first, second = product[:, :128], product[:, 128:]
                if mine == 3:
                    through = 2 * size + k
                    x_sums[through].wait_recv()
                    if k % 2 == 0:
                        second = second + xr[through].astype(F32)
                    else:
                        first = first + xr[through].astype(F32)
                    push(3 * size + k, first, p1_same)
                    push(4 * size + k, second, p2_same)
                else:
                    keep[mine * size + k] = first
                    push(mine * size + k, second, (p2_same, p1_same, p2_same if k % 2 else p1_same)[mine])

    y_sums = {}
    own_total = None
    with jax.named_scope("x_sum"):
        for mine in (0, 1, 2):
            for k in range(size):
                slot = mine * size + k
                total = keep[slot]
                for source in (3 * size + k, 4 * size + k) if mine == 2 else (slot,):
                    x_sums[source].wait_recv()
                    total = total + xr[source].astype(F32)
                distance = distances[mine][k]
                if mine < 2 and distance == 0:
                    own_total = total
                else:
                    ys[slot] = total.astype(BF16)
                    y_sums[slot] = remote(
                        ys.at[slot], yr.at[slot], y_send.at[0], y_recv.at[slot], y_dev(distance)
                    )
                    y_sums[slot].start()
    with jax.named_scope("y_sum"):
        for slot in y_sums:
            y_sums[slot].wait_recv()
            own_total = own_total + yr[slot].astype(F32)

    chunk = 128 // owners
    zsrc[...] = own_total.T.astype(BF16)
    owner = z < owners
    quarter = c * 2 + l
    peers = (p1_same, p1_other, core_dev)

    def z_sum(d):
        there = lax.rem(z + d, nz)
        place = pl.ds(pl.multiple_of(there * chunk, 16), chunk)
        return there < owners, remote(zsrc.at[place, :], zr.at[d], zr_send.at[0], zr_recv.at[0], z_dev(d))

    def chunk_of(at):
        return fin.at[pl.ds(pl.multiple_of(quarter * 128 + at * chunk, 16), chunk), :]

    def z_all(d):
        return remote(chunk_of(z), chunk_of(z), za_send.at[0], za_recv.at[d], z_dev(d))

    def hand_on(at):
        for k, device in enumerate(peers):
            remote(chunk_of(at), chunk_of(at), f_send.at[k], f_recv.at[k], device).start()

    with jax.named_scope("z_sum"):
        for d in z_order:
            wanted, copy = z_sum(d)
            pl.when(wanted)(copy.start)

        @pl.when(owner)
        def _():
            piece = zsrc[pl.ds(pl.multiple_of(z * chunk, 16), chunk), :].astype(F32)
            arrived = zr.at[pl.ds(1, nz - 1)]
            remote(arrived, arrived, zr_send.at[0], zr_recv.at[0], z_dev(1)).wait_recv()
            for d in z_order:
                piece = piece + zr[d].astype(F32)
            fin[pl.ds(pl.multiple_of(quarter * 128 + z * chunk, 16), chunk), :] = piece.astype(BF16)
            for d in z_order:
                z_all(d).start()
            hand_on(z)

    with jax.named_scope("z_all"):
        for d in reversed(z_order):
            source = lax.rem(z - d + nz, nz)

            @pl.when(source < owners)
            def _():
                arrived = chunk_of(source)
                remote(arrived, arrived, za_send.at[0], za_recv.at[d], z_dev(d)).wait_recv()
                hand_on(source)

    with jax.named_scope("end_wait"):
        for k, (cc, ll) in enumerate(((c, 1 - l), (1 - c, 1 - l), (1 - c, l))):
            theirs = fin.at[pl.ds(pl.multiple_of((cc * 2 + ll) * 128, 128), 128), :]
            remote(theirs, theirs, f_send.at[k], f_recv.at[k], peers[k]).wait_recv()
    gw_out[...] = fin[...]

    with jax.named_scope("send_waits"):
        own_quarter = fin.at[pl.ds(pl.multiple_of(quarter * 128, 128), 128), :]
        for k, device in enumerate(peers):
            remote(own_quarter, own_quarter, f_send.at[k], f_recv.at[k], device).wait_send()
        for sends, count in ((owner, owners - 1), (jnp.logical_not(owner), owners)):
            if count:
                sent = zr.at[pl.ds(0, count)]
                pl.when(sends)(remote(sent, sent, zr_send.at[0], zr_recv.at[0], z_dev(1)).wait_send)
        sent = zr.at[pl.ds(1, nz - 1)]
        pl.when(owner)(remote(sent, sent, za_send.at[0], za_recv.at[0], z_dev(1)).wait_send)
        for copies in (kv_copies.values(), grad_copies.values()):
            for copy in copies:
                copy.wait_send()
        sent = gs.at[pl.ds(tok, 9 * tok), :]
        remote(sent, sent, g_send.at[0], g_recv.at[1], core_dev).wait_send()
        remote(xs, xs, xs_send.at[0], xs_recv.at[0], core_dev).wait_send()
        sent = ys.at[pl.ds(0, len(y_sums))]
        remote(sent, sent, y_send.at[0], y_recv.at[0], y_dev(1)).wait_send()
        for k, sent in enumerate((from_same, from_other, from_core)):
            remote(sent, sent, xsnd.at[k], xrcv.at[0], core_dev).wait_send()


def write_results(dq_in, gkv_in, gw_in, dq_out, gkv_out, gw_out, wide, sems):
    copies = [
        pltpu.make_async_copy(dq_in, dq_out, sems.at[0]),
        pltpu.make_async_copy(gkv_in, gkv_out, sems.at[1]),
        pltpu.make_async_copy(wide, gw_out, sems.at[2]),
    ]
    copies[0].start()
    copies[1].start()
    wide[...] = gw_in[...].astype(F32)
    copies[2].start()
    for copy in copies:
        copy.wait()


def local(ny, nz, layer_input, query, keys_values, grad_output, logsumexp, delta):
    tok = query.shape[0]
    heads = HQ * tok
    lists = ((3, 0), (6, 7), (4, 1), (5, 2)) if ny == 8 else ((0,), (3,), (2,), (1,))
    size = len(lists[0])
    owners = 8 if nz >= 8 else nz // 2
    dma = pltpu.SemaphoreType.DMA
    any_spec = pl.BlockSpec(memory_space=pl.ANY)
    vmem_spec = pl.BlockSpec(memory_space=pltpu.VMEM)
    results = pl.pallas_call(
        functools.partial(kernel, ny, nz, tok, lists, owners),
        out_shape=(
            pltpu.VMEM((tok, HQ * HD), BF16),
            pltpu.VMEM((tok, 2 * HD), BF16),
            pltpu.VMEM((512, 2 * HD), BF16),
        ),
        in_specs=[any_spec] * 6,
        out_specs=(vmem_spec, vmem_spec, vmem_spec),
        scratch_shapes=[
            pltpu.VMEM((heads, HD), BF16),
            pltpu.VMEM((heads, HD), BF16),
            pltpu.VMEM((HQ, tok), F32),
            pltpu.VMEM((HQ, tok), F32),
            pltpu.VMEM((16, heads), F32),
            pltpu.VMEM((WIN + 2, tok, 2 * HD), BF16),
            pltpu.VMEM(((WIN + 2) * tok, heads), BF16),
            pltpu.VMEM((WIN + 1, tok, 2 * HD), BF16),
            pltpu.VMEM((WIN + 1, tok, 2 * HD), BF16),
            pltpu.VMEM((4, 2 * tok, size * 256), BF16),
            pltpu.VMEM((4, 2 * tok, size * 256), BF16),
            pltpu.VMEM((10 * tok, 2 * HD), BF16),
            pltpu.VMEM((2 * HD, 10 * tok), BF16),
            pltpu.VMEM((3 * size, 256, 128), F32),
            pltpu.VMEM((5 * size, 256, 128), BF16),
            pltpu.VMEM((5 * size, 256, 128), BF16),
            pltpu.VMEM((3 * size, 256, 128), BF16),
            pltpu.VMEM((3 * size, 256, 128), BF16),
            pltpu.VMEM((128, 2 * HD), BF16),
            pltpu.VMEM((nz, 128 // owners, 2 * HD), BF16),
            pltpu.VMEM((512, 2 * HD), BF16),
            dma((5,)),
            dma((1,)),
            dma((WIN + 1,)),
            dma((WIN + 1,)),
            dma((WIN + 1,)),
            dma((WIN + 1,)),
            dma((3,)),
            dma((5,)),
            dma((1,)),
            dma((10,)),
            dma((1,)),
            dma((5 * size,)),
            dma((1,)),
            dma((3 * size,)),
            dma((1,)),
            dma((1,)),
            dma((1,)),
            dma((nz,)),
            dma((3,)),
            dma((3,)),
        ],
        compiler_params=pltpu.CompilerParams(
            collective_id=0, has_side_effects=True, vmem_limit_bytes=56 * 1024 * 1024
        ),
    )(layer_input, query, keys_values, grad_output, logsumexp.T, delta.T)
    return pl.pallas_call(
        write_results,
        out_shape=(
            jax.ShapeDtypeStruct((tok, HQ * HD), BF16),
            jax.ShapeDtypeStruct((tok, 2 * HD), BF16),
            jax.ShapeDtypeStruct((512, 2 * HD), F32),
        ),
        in_specs=[vmem_spec] * 3,
        out_specs=(any_spec, any_spec, any_spec),
        scratch_shapes=[pltpu.VMEM((512, 2 * HD), F32), dma((3,))],
    )(*[pltpu.with_memory_space_constraint(result, pltpu.VMEM) for result in results])


def solution(mesh):
    ny = mesh.shape["outer"] // 2
    nz = mesh.shape["inner"] // 4
    finer = Mesh(mesh.devices.reshape(2, ny, nz, 2, 2), AXES)
    tokens = P(AXES, None)
    return jax.shard_map(
        functools.partial(local, ny, nz),
        mesh=finer,
        in_specs=(tokens,) * 6,
        out_specs=(tokens, tokens, P(("x_hi", "y"), None)),
        check_vma=False,
    )
```

time: 96.3 us -> 74 us (0.77)
  Pallas kernels: 90.4 us -> 73.2 us
  local copies, waits for them, and re-layouts: 3.3 us -> 0 us
  other arithmetic: 1.78 us -> 0 us
    pallas_call x1 -> x2, Pallas kernels: 90.4 us -> 73.2 us  [the longest x1 72.2 us: local(): pl.pallas_call(functools.partial(kernel, ny, nz, tok, lists, owners), out...]
    unnamed x2 -> x0, local copies, waits for them, and re-layouts: 3.3 us -> none
    convert_element_type x1 -> x0, other arithmetic: 1.78 us -> none  [local(): return (grad_query, grad_kv, grad_weight.astype(F32))]
where the time goes in v2:
time: 74 us; the launch traced here: 73.8 us
  Pallas kernels  73.2 us (99%)
    pallas_call x1, Pallas kernels, local(): pl.pallas_call(functools.partial(kernel, ny, nz, tok, lists, owners), out...  72.2 us

profile of v2, /device:TPU:1, one launch (start us, length us, event | category | flops | bytes accessed | tf_op | source)
XLA Modules:
  0.0 73.8 jit_solution(13466541169579712412)
XLA Ops:
  0.6 72.2 %shard_map.85 = (bf16[192,1024]{1,0:T(8,128)(2,1)S(1)}, bf16[192,256]{1,0:T(8,128)(2,1)S(1)}, bf16[512,256]{1,0:T(8,128)(2,1)S(1)}) custom-call(bf16[192,8192]{1,0:T(8,128)(2,1)} %x_hbm.1, bf16[192,1024]{1,0:T(8,128)(2,1)} %q_hbm.1, bf16[192,256]{1,0:T(8,128)(2,1)} %kv_hbm.1, bf16[192,1024]{1,0:T(8,128)(2,1)} %do_hbm.1, f32[8,192]{1,0:T(8,128)} %bitcast.2, ...), custom_call_target="tpu_custom_call" | custom-call | tf_op jit(solution)/shard_map/pallas_call | solution.py:429
  72.9 1.0 %shard_map.86 = (bf16[192,1024]{1,0:T(8,128)(2,1)}, bf16[192,256]{1,0:T(8,128)(2,1)}, f32[512,256]{1,0:T(8,128)}) custom-call(bf16[192,1024]{1,0:T(8,128)(2,1)S(1)} %get-tuple-element.6.dq_in, bf16[192,256]{1,0:T(8,128)(2,1)S(1)} %get-tuple-element.7.gkv_in, bf16[512,256]{1,0:T(8,128)(2,1)S(1)} %get-tuple-element.8.gw_in), custom_call_target="tpu_custom_call" | custom-call | tf_op jit(solution)/shard_map/pallas_call | solution.py:485

commit v3 on v2

--- a/solution.py
+++ b/solution.py
@@ -172,7 +172,7 @@
         rows[8:9, k * tok : (k + 1) * tok] = delta_in[k : k + 1, :]
 
     wide = 2 * tok
-    heads = HQ // 2
+    heads = HQ
     key_pos = lax.broadcasted_iota(jnp.int32, (tok, heads * tok), 0)
     lane = lax.broadcasted_iota(jnp.int32, (tok, heads * tok), 1)
     causal = key_pos <= lax.rem(lane, tok)
@@ -420,7 +420,7 @@
 def local(ny, nz, layer_input, query, keys_values, grad_output, logsumexp, delta):
     tok = query.shape[0]
     heads = HQ * tok
-    lists = ((3, 0), (6, 7), (4, 1), (5, 2)) if ny == 8 else ((0,), (3,), (2,), (1,))
+    lists = ((6, 0), (7, 1), (4, 2), (3, 5)) if ny == 8 else ((0,), (3,), (2,), (1,))
     size = len(lists[0])
     owners = 8 if nz >= 8 else nz // 2
     dma = pltpu.SemaphoreType.DMA

time: 74 us -> 73.4 us (level)
  Pallas kernels: 73.2 us -> 72.3 us
    pallas_call x1, Pallas kernels: 72.2 us -> 71.4 us  [local(): pl.pallas_call(functools.partial(kernel, ny, nz, tok, lists, owners), out...]
where the time goes in v3:
time: 73.4 us; the launch traced here: 73 us
  Pallas kernels  72.3 us (99%)
    pallas_call x1, Pallas kernels, local(): pl.pallas_call(functools.partial(kernel, ny, nz, tok, lists, owners), out...  71.4 us

profile of v3, /device:TPU:1, one launch (start us, length us, event | category | flops | bytes accessed | tf_op | source)
XLA Modules:
  0.0 73.0 jit_solution(8091441284344682668)
XLA Ops:
  0.6 71.4 %shard_map.85 = (bf16[192,1024]{1,0:T(8,128)(2,1)S(1)}, bf16[192,256]{1,0:T(8,128)(2,1)S(1)}, bf16[512,256]{1,0:T(8,128)(2,1)S(1)}) custom-call(bf16[192,8192]{1,0:T(8,128)(2,1)} %x_hbm.1, bf16[192,1024]{1,0:T(8,128)(2,1)} %q_hbm.1, bf16[192,256]{1,0:T(8,128)(2,1)} %kv_hbm.1, bf16[192,1024]{1,0:T(8,128)(2,1)} %do_hbm.1, f32[8,192]{1,0:T(8,128)} %bitcast.2, ...), custom_call_target="tpu_custom_call" | custom-call | tf_op jit(solution)/shard_map/pallas_call | solution.py:429
  72.0 1.0 %shard_map.86 = (bf16[192,1024]{1,0:T(8,128)(2,1)}, bf16[192,256]{1,0:T(8,128)(2,1)}, f32[512,256]{1,0:T(8,128)}) custom-call(bf16[192,1024]{1,0:T(8,128)(2,1)S(1)} %get-tuple-element.6.dq_in, bf16[192,256]{1,0:T(8,128)(2,1)S(1)} %get-tuple-element.7.gkv_in, bf16[512,256]{1,0:T(8,128)(2,1)S(1)} %get-tuple-element.8.gw_in), custom_call_target="tpu_custom_call" | custom-call | tf_op jit(solution)/shard_map/pallas_call | solution.py:485
